TPU v7x, 32 devices: a whole 2x2x4 slice. The times are simulated.
32 devices in a mesh: tile: 8 (over z, x), trc: 4 (over y, core).
Axes of the slice: x: 2, y: 2, z: 4, core: 2. Of those that a mesh axis runs over, the one named last changes fastest.
Arguments:
- tracers: float32 [256, 4, 32, 128], P('trc', None, 'tile'), may hold values from 0.1 to 4
- courant_cycle: float32 [4, 32, 128], P(None, 'tile'), may hold values from -0.45 to 0.45
- courant_edge: float32 [4, 32, 128], P(None, 'tile'), may hold values from -0.45 to 0.45
- seam_flags: int32 [8, 2], P('tile'), may hold values from 0 to 1, as said below
- sunlit: int32 [32, 128], P('tile', 'trc'), may hold values from 0 to 1, as said below
- table_entry: int32 [4, 4, 32, 128], P(None, None, 'tile', 'trc'), may hold values from 0 to 3
- linear_maps: bfloat16 [4, 256, 256], replicated, may hold values from -0.375 to 0.375
- offsets: float32 [4, 256], replicated, may hold values from -4 to 4
- mixing: float32 [3, 32, 128], P(None, 'tile', 'trc'), may hold values from 0.05 to 5
Outputs:
- tracers_out: float32 [256, 4, 32, 128], P('trc', None, 'tile')
Inputs may be any that keep to these rules, and one draw needn't show every extreme that they name: seam_flags[t, 1] equals seam_flags[t + 1, 0] (tile numbers mod 8); a flag is 1 only on the edge before a tile whose number is a multiple of 2, and at least one flag is 1. In every row of the edge-cell dimension, cycle column x is sunlit exactly when cycle column x + 32 / 2 (mod 32) is not; some tile is sunlit in all of its columns.
All inputs are finite; a program needn't handle non-finite values.
Results may differ from a plain program's by a relative error of at most 0.0025.
Values may be sent and summed in bfloat16 or wider, within the bound.
A program may use at most 64 MiB of HBM per device.

v0:
```python
import jax
import jax.numpy as jnp
from jax import lax
from jax.sharding import PartitionSpec as P

block_boxes = 128


def padded_2(block, sides, width):
    for axis, dim in sides:
        count = lax.axis_size(axis)
        forward = [(i, i + 1) for i in range(count - 1)]
        forward.append((count - 1, 0))
        backward = [(target, source) for source, target in forward]
        low = lax.ppermute(
            lax.slice_in_dim(block, block.shape[dim] - width, None, axis=dim), axis, forward
        )
        high = lax.ppermute(lax.slice_in_dim(block, 0, width, axis=dim), axis, backward)
        block = jnp.concatenate([low, block, high], axis=dim)
    return block


def cut_range(values, start, stop, direction):
    return lax.slice_in_dim(values, start, stop, axis=direction)


def edge_values(stencil, direction):
    length = stencil.shape[direction]
    inner_sum = cut_range(stencil, 1, length - 2, direction) + cut_range(
        stencil, 2, length - 1, direction
    )
    outer_sum = cut_range(stencil, 0, length - 3, direction) + cut_range(
        stencil, 3, length, direction
    )
    return 7.0 / 12.0 * inner_sum - 1.0 / 12.0 * outer_sum


def sweep_flux(stencil, courant, direction):
    inside = stencil.shape[direction] - 6
    edge_vals = edge_values(stencil, direction)
    left_pos = cut_range(edge_vals, 0, inside + 1, direction)
    middle = cut_range(edge_vals, 1, inside + 2, direction)
    right_neg = cut_range(edge_vals, 2, inside + 3, direction)
    center_pos = cut_range(stencil, 2, inside + 3, direction)
    center_neg = cut_range(stencil, 3, inside + 4, direction)
    curve_pos = 6.0 * center_pos - 3.0 * (left_pos + middle)
    flux_pos = courant * (
        middle - 0.5 * courant * (middle - left_pos - (1.0 - 2.0 * courant / 3.0) * curve_pos)
    )
    reverse_speed = -courant
    curve_neg = 6.0 * center_neg - 3.0 * (middle + right_neg)
    flux_neg = courant * (
        middle
        + 0.5 * reverse_speed * (right_neg - middle + (1.0 - 2.0 * reverse_speed / 3.0) * curve_neg)
    )
    return jnp.where(courant > 0.0, flux_pos, flux_neg)


def tendency(flux, direction):
    length = flux.shape[direction]
    return cut_range(flux, 0, length - 1, direction) - cut_range(flux, 1, length, direction)


def wall_faces(courant_edge):
    closed = jnp.zeros(courant_edge.shape[:-1] + (1,), jnp.float32)
    return jnp.concatenate([closed, courant_edge[..., 1:], closed], axis=-1)


def edge_sweep(tracers, courant_edge):
    stencil = jnp.pad(tracers, ((0, 0), (0, 0), (0, 0), (3, 3)), mode="edge")
    return tendency(sweep_flux(stencil, wall_faces(courant_edge)[None], 3), 3)


def solve_columns(values, coupling):
    levels = values.shape[1]
    zero_row = jnp.zeros(values.shape[2:], jnp.float32)
    ratio_list = []
    solved_list = []
    for level_index in range(levels):
        coupling_below = coupling[level_index - 1] if level_index > 0 else zero_row
        coupling_above = coupling[level_index] if level_index < levels - 1 else zero_row
        diagonal = 1.0 + coupling_below + coupling_above
        if level_index == 0:
            pivot_value = diagonal
            current = values[:, 0] / pivot_value
        else:
            pivot_value = diagonal - coupling_below * ratio_list[-1]
            current = (values[:, level_index] + coupling_below * solved_list[-1]) / pivot_value
        ratio_list.append(coupling_above / pivot_value)
        solved_list.append(current)
    result_list = [solved_list[-1]]
    for level_index in range(levels - 2, -1, -1):
        result_list.append(solved_list[level_index] + ratio_list[level_index] * result_list[-1])
    return jnp.stack(result_list[::-1], axis=1)


def orient(block_cells, reverse_flag):
    return jnp.where(reverse_flag > 0, block_cells[..., ::-1], block_cells)


def grouped_maps(values, entry_ids, linear_maps, offsets):
    species, box_count = values.shape
    entries = linear_maps.shape[0]
    member = (entry_ids[:, None] == jnp.arange(entries, dtype=jnp.int32)[None, :]).astype(jnp.int32)
    counts = jnp.sum(member, axis=0)
    padded = (counts + block_boxes - 1) // block_boxes * block_boxes
    group_end = jnp.cumsum(padded)
    group_start = group_end - padded
    within = jnp.sum((jnp.cumsum(member, axis=0) - 1) * member, axis=1)
    target = jnp.sum(member * group_start[None, :], axis=1) + within
    capacity = (box_count + block_boxes - 1) // block_boxes * block_boxes + entries * block_boxes
    buffer = jnp.zeros((species, capacity), jnp.bfloat16).at[:, target].set(values)
    tile_count = capacity // block_boxes
    tile_start = jnp.arange(tile_count, dtype=jnp.int32) * block_boxes
    tile_entry = jnp.minimum(
        jnp.sum((group_end[None, :] <= tile_start[:, None]).astype(jnp.int32), axis=1), entries - 1
    )
    chosen = jnp.take(linear_maps, tile_entry, axis=0)
    product = jnp.einsum(
        "toi,itb->otb",
        chosen,
        buffer.reshape(species, tile_count, block_boxes),
        preferred_element_type=jnp.float32,
    )
    gathered = jnp.take(product.reshape(species, capacity), target, axis=1)
    shift_terms = jnp.dot(offsets.T, member.T.astype(jnp.float32), precision=lax.Precision.HIGHEST)
    return gathered + shift_terms


def chemistry_steps(work_boxes, work_entry, linear_maps, offsets):
    species, levels, columns = work_boxes.shape
    chem_input = work_boxes.reshape(species, levels * columns)
    result = chem_input.astype(jnp.float32)
    for substep in range(work_entry.shape[0]):
        result = jnp.maximum(
            grouped_maps(
                chem_input, work_entry[substep].reshape(levels * columns), linear_maps, offsets
            ),
            0.0,
        )
        chem_input = result.astype(jnp.bfloat16)
    return result.reshape(species, levels, columns)


def shards(
    tracers,
    courant_cycle,
    courant_edge,
    seam_flags,
    sunlit,
    table_entry,
    linear_maps,
    offsets,
    mixing,
):
    quarter, levels, tile_width, edge_length = tracers.shape
    stacked = jnp.concatenate([tracers, courant_cycle[None]], axis=0)
    padded = padded_2(stacked, (("tile", 2),), 3)
    before = orient(padded[:, :, :3, :], seam_flags[0, 0])
    after_cols = orient(padded[:, :, tile_width + 3 :, :], seam_flags[0, 1])
    stencil = jnp.concatenate([before[:quarter], tracers, after_cols[:quarter]], axis=2)
    cycle_faces = jnp.concatenate([courant_cycle, after_cols[quarter][:, :1, :]], axis=1)
    edge_part = edge_sweep(tracers, courant_edge)
    cycle_part = tendency(sweep_flux(stencil, cycle_faces[None], 2), 2)
    advected = tracers + cycle_part + edge_part
    rounded = advected.astype(jnp.bfloat16)
    box_data = lax.all_to_all(rounded, "trc", split_axis=3, concat_axis=0, tiled=True)
    species = box_data.shape[0]
    columns = tile_width * box_data.shape[3]
    box_data = box_data.reshape(species, levels, columns)
    entry_cols = table_entry.reshape(table_entry.shape[0], levels, columns)
    daylit = sunlit.reshape(columns)
    changed = chemistry_steps(box_data, entry_cols, linear_maps, offsets)
    chem_out = jnp.where(daylit[None, None, :] > 0, changed, box_data.astype(jnp.float32))
    mixed_out = solve_columns(chem_out, mixing.reshape(levels - 1, columns))
    tracer_back = mixed_out.reshape(species, levels, tile_width, columns // tile_width)
    return lax.all_to_all(tracer_back, "trc", split_axis=0, concat_axis=3, tiled=True)


def solution(mesh):
    placed = (
        P("trc", None, "tile", None),
        P(None, "tile", None),
        P(None, "tile", None),
        P("tile", None),
        P("tile", "trc"),
        P(None, None, "tile", "trc"),
        P(),
        P(),
        P(None, "tile", "trc"),
    )
    return jax.shard_map(
        shards, mesh=mesh, in_specs=placed, out_specs=P("trc", None, "tile", None), check_vma=False
    )
```

profile of v0, /device:TPU:0, one launch (start us, length us, event | category | flops | bytes accessed | tf_op | source)
XLA Modules:
  0.0 155.3 jit_solution(3080743185110450820)
XLA Ops:
  3.0 6.0 %collective-permute-start = (f32[65,4,3,128]{3,1,2,0:T(4,128)}, f32[65,4,3,128]{3,1,2,0:T(4,128)S(1)}, u32[]{:S(2)}, u32[]{:S(2)}) collective-permute-start(f32[65,4,3,128]{3,1,2,0:T(4,128)} %get-tuple-element.46), channel_id=1, source_target_pairs={{4,0},{8,4},{12,8},{16,12},{20,16},{24,20},{28,24},{0,28},{5,1},{9... | collective-permute-start | bytes 1198088 | tf_op jit(solution)/shard_map/ppermute | solution.py:18
  35.6 1.6 %gather_fusion = bf16[8,256,256]{2,1,0:T(8,128)(2,1)} fusion(bf16[4,256,256]{2,1,0:T(8,128)(2,1)S(1)} %copy-done, s32[1024]{0:T(1024)S(1)} %pad_clamp_fusion.7), kind=kCustom, calls=%fused_computation.clone | custom fusion | bytes 2097184 | tf_op jit(solution)/shard_map/jit(_take)/gather | solution.py:118
  37.3 1.6 %gather_fusion.2 = bf16[8,256,256]{2,1,0:T(8,128)(2,1)} fusion(bf16[4,256,256]{2,1,0:T(8,128)(2,1)S(1)} %copy-done, s32[1024]{0:T(1024)S(1)} %pad_clamp_fusion.5), kind=kCustom, calls=%fused_computation.2.clone | custom fusion | bytes 2097184 | tf_op jit(solution)/shard_map/jit(_take)/gather | solution.py:118
  41.2 1.6 %gather_fusion.4 = bf16[8,256,256]{2,1,0:T(8,128)(2,1)} fusion(bf16[4,256,256]{2,1,0:T(8,128)(2,1)S(1)} %copy-done, s32[1024]{0:T(1024)S(1)} %pad_clamp_fusion.3), kind=kCustom, calls=%fused_computation.3.clone | custom fusion | bytes 2097184 | tf_op jit(solution)/shard_map/jit(_take)/gather | solution.py:118
  49.5 8.3 %multiply_select_fusion = f32[64,4,4,129]{0,2,1,3:T(4,128)} fusion(f32[64,4,4,3]{0,2,1,3:T(4,128)S(1)} %reshape.1150, f32[64,4,4,131]{0,2,1,3:T(4,128)S(1)} %fusion.37, f32[64,4,4,3]{0,2,1,3:T(4,128)S(1)} %reshape.1149, f32[64,4,4,128]{0,2,1,3:T(4,128)S(1)} %copy.171, f32[4,4,129]{1,0,2:T(4,128)} %copy.182, f32[4,4,129]{1,0,2:T(4,128)} %copy.181, ...), kind=kLoop, calls=%fused_computation.83 | loop fusion | flops 3038208 | bytes 2705744 | tf_op jit(solution)/shard_map/jit(_where)/select_n | solution.py:56
  60.5 2.2 %rev.7 = f32[65,4,3,128]{3,1,2,0:T(4,128)S(1)} reverse(f32[65,4,3,128]{3,1,2,0:T(4,128)} %collective-permute-done.1), dimensions={3} | reverse | bytes 798720 | tf_op jit(solution)/shard_map/rev | solution.py:98
  65.2 2.5 %pad_maximum_fusion = f32[64,4,10,128]{0,2,1,3:T(8,128)S(1)} fusion(f32[64,4,3,128]{0,2,1,3:T(4,128)S(1)} %copy.162, f32[64,4,4,128]{0,2,1,3:T(4,128)S(1)} %copy.171, f32[64,4,3,128]{0,2,1,3:T(4,128)} %copy.160), kind=kLoop, calls=%fused_computation.12 | loop fusion | flops 655360 | bytes 2621440 | tf_op jit(solution)/shard_map/concatenate | solution.py:161
  67.8 3.0 %fusion.11 = f32[64,4,7,128]{0,2,1,3:T(8,128)} fusion(f32[64,4,3,128]{0,2,1,3:T(4,128)S(1)} %copy.162, f32[64,4,4,128]{0,2,1,3:T(4,128)S(1)} %copy.171, f32[64,4,3,128]{0,2,1,3:T(4,128)S(1)} %copy-done.1, f32[64,4,10,128]{0,2,1,3:T(8,128)S(1)} %pad_maximum_fusion), kind=kLoop, calls=%fused_computation.30 | loop fusion | flops 1605632 | bytes 4063232 | tf_op jit(solution)/shard_map/sub | solution.py:35
  73.2 8.3 %fusion.8 = f32[64,4,5,128]{0,2,1,3:T(8,128)S(1)} fusion(f32[64,4,4,128]{0,2,1,3:T(4,128)S(1)} %copy.171, f32[64,4,3,128]{0,2,1,3:T(4,128)S(1)} %copy.162, f32[64,4,3,128]{0,2,1,3:T(4,128)} %copy.160, f32[64,4,7,128]{0,2,1,3:T(8,128)} %fusion.11, f32[4,5,128]{1,0,2:T(4,128)} %copy.170, f32[4,5,128]{1,0,2:T(4,128)} %copy.169, f32[4,5,128]{1,0,2:T(4,128)S(1)} %copy.168, ...), kind=kLoop, calls=%fused_computation.27 | loop fusion | flops 3768320 | bytes 3985920 | tf_op jit(solution)/shard_map/jit(_where)/select_n | solution.py:56
  83.2 3.6 %all-to-all-start = ((bf16[4,2,16384]{2,1,0:T(2,128)(2,1)}), bf16[4,2,16384]{2,1,0:T(2,128)(2,1)S(1)}, u32[]{:S(2)}, u32[]{:S(2)}) async-start(bf16[4,2,16384]{2,1,0:T(2,128)(2,1)} %reshape.1293), calls=%async_computation | async-start | bytes 524288 | tf_op jit(solution)/shard_map/all_to_all | solution.py:167
  86.9 5.8 %all-to-all-done = bf16[4,2,16384]{2,1,0:T(2,128)(2,1)S(1)} async-done(((bf16[4,2,16384]{2,1,0:T(2,128)(2,1)}), bf16[4,2,16384]{2,1,0:T(2,128)(2,1)S(1)}, u32[]{:S(2)}, u32[]{:S(2)}) %all-to-all-start) | async-done | bytes 262176 | tf_op jit(solution)/shard_map/all_to_all | solution.py:167
  95.1 1.8 %reshape.1160 = f32[256,4,128]{0,2,1:T(8,128)S(1)} reshape(f32[4,64,4,4,32]{1,0,4,3,2:T(4,128)} %copy.185) | data formatting | bytes 1048576 | tf_op jit(solution)/shard_map/convert_element_type | solution.py:174
  96.9 3.3 %scatter_custom_fusion = bf16[256,1024]{0,1:T(8,128)(2,1)} fusion(s32[512]{0:T(512)} %bitcast.249, bf16[256,512]{0,1:T(8,128)(2,1)S(1)} %reshape.1226, bf16[]{:T(256)} %constant.130.clone.1), kind=kCustom, calls=%fused_computation.108 | custom fusion | bytes 786944 | tf_op jit(solution)/shard_map/scatter | solution.py:112
  100.2 1.6 %fusion.62 = f32[8,128,256]{2,1,0:T(8,128)S(1)} fusion(bf16[256,8,128]{0,2,1:T(8,128)(2,1)} %bitcast.232, bf16[8,256,256]{2,1,0:T(8,128)(2,1)S(1)} %copy-done.6, pred[8]{0:T(512)(128)(4,1)S(1)} %copy-done.54), kind=kOutput, calls=%fused_computation.95 | convolution fusion | flops 134742016 | bytes 2621448 | tf_op jit(solution)/shard_map/toi,itb->otb/dot_general | solution.py:119
  101.8 2.2 %gather_fusion.1 = f32[512,256]{1,0:T(8,128)} fusion(f32[256,1024]{0,1:T(8,128)S(1)} %bitcast.222, s32[1024]{0:T(1024)S(1)} %copy-done.29), kind=kCustom, calls=%fused_computation.1.clone | custom fusion | bytes 1050624 | tf_op jit(solution)/shard_map/jit(_take)/gather | solution.py:125
  104.1 1.7 %fusion.34 = bf16[512,256]{1,0:T(8,128)(2,1)S(1)} fusion(f32[4,256]{1,0:T(4,128)S(1)} %copy-done.8, f32[512,256]{1,0:T(8,128)} %gather_fusion.1, pred[512]{0:T(512)(128)(4,1)S(1)} %copy-done.50, s32[512]{0:T(512)S(1)} %copy-done.21), kind=kOutput, calls=%fused_computation.62 | convolution fusion | flops 6821888 | bytes 793088 | tf_op jit(solution)/shard_map/dot_general | solution.py:126
  105.8 3.3 %scatter_custom_fusion.1 = bf16[256,1024]{0,1:T(8,128)(2,1)} fusion(s32[512]{0:T(512)} %bitcast.250, bf16[512,256]{1,0:T(8,128)(2,1)S(1)} %fusion.34, bf16[]{:T(256)} %constant.130.clone.1), kind=kCustom, calls=%fused_computation.114 | custom fusion | bytes 524800 | tf_op jit(solution)/shard_map/scatter | solution.py:112
  109.0 1.6 %fusion.60 = f32[8,128,256]{2,1,0:T(8,128)S(1)} fusion(bf16[256,8,128]{0,2,1:T(8,128)(2,1)} %bitcast.231, bf16[8,256,256]{2,1,0:T(8,128)(2,1)S(1)} %copy-done.4, pred[8]{0:T(512)(128)(4,1)S(1)} %copy-done.53), kind=kOutput, calls=%fused_computation.93 | convolution fusion | flops 134742016 | bytes 2621448 | tf_op jit(solution)/shard_map/toi,itb->otb/dot_general | solution.py:119
  110.7 2.2 %gather_fusion.3 = f32[512,256]{1,0:T(8,128)} fusion(f32[256,1024]{0,1:T(8,128)S(1)} %bitcast.220, s32[1024]{0:T(1024)S(1)} %copy-done.28), kind=kCustom, calls=%fused_computation.5.clone | custom fusion | bytes 1050624 | tf_op jit(solution)/shard_map/jit(_take)/gather | solution.py:125
  112.9 1.7 %fusion.33 = bf16[512,256]{1,0:T(8,128)(2,1)S(1)} fusion(f32[4,256]{1,0:T(4,128)S(1)} %copy-done.8, f32[512,256]{1,0:T(8,128)} %gather_fusion.3, pred[512]{0:T(512)(128)(4,1)S(1)} %copy-done.51, s32[512]{0:T(512)S(1)} %copy-done.19), kind=kOutput, calls=%fused_computation.61 | convolution fusion | flops 6821888 | bytes 793088 | tf_op jit(solution)/shard_map/dot_general | solution.py:126
  114.6 3.3 %scatter_custom_fusion.2 = bf16[256,1024]{0,1:T(8,128)(2,1)} fusion(s32[512]{0:T(512)} %bitcast.251, bf16[512,256]{1,0:T(8,128)(2,1)S(1)} %fusion.33, bf16[]{:T(256)} %constant.130.clone.1), kind=kCustom, calls=%fused_computation.112 | custom fusion | bytes 524800 | tf_op jit(solution)/shard_map/scatter | solution.py:112
  117.9 1.6 %fusion.58 = f32[8,128,256]{2,1,0:T(8,128)S(1)} fusion(bf16[256,8,128]{0,2,1:T(8,128)(2,1)} %bitcast.233, bf16[8,256,256]{2,1,0:T(8,128)(2,1)S(1)} %copy-done.5, pred[8]{0:T(512)(128)(4,1)S(1)} %copy-done.56), kind=kOutput, calls=%fused_computation.91 | convolution fusion | flops 134742016 | bytes 2621448 | tf_op jit(solution)/shard_map/toi,itb->otb/dot_general | solution.py:119
  119.5 2.5 %gather_fusion.5 = f32[512,256]{1,0:T(8,128)} fusion(f32[256,1024]{0,1:T(8,128)S(1)} %bitcast.223, s32[1024]{0:T(1024)S(1)} %copy-done.27), kind=kCustom, calls=%fused_computation.6.clone | custom fusion | bytes 1050624 | tf_op jit(solution)/shard_map/jit(_take)/gather | solution.py:125
  122.0 1.7 %fusion.32 = bf16[512,256]{1,0:T(8,128)(2,1)S(1)} fusion(f32[4,256]{1,0:T(4,128)S(1)} %copy-done.8, f32[512,256]{1,0:T(8,128)} %gather_fusion.5, pred[512]{0:T(512)(128)(4,1)S(1)} %copy-done.52, s32[512]{0:T(512)S(1)} %copy-done.17), kind=kOutput, calls=%fused_computation.60 | convolution fusion | flops 6821888 | bytes 793088 | tf_op jit(solution)/shard_map/dot_general | solution.py:126
  123.7 3.1 %scatter_custom_fusion.3 = bf16[256,1024]{0,1:T(8,128)(2,1)} fusion(s32[512]{0:T(512)S(1)} %bitcast.252, bf16[512,256]{1,0:T(8,128)(2,1)S(1)} %fusion.32, bf16[]{:T(256)} %constant.130.clone.1), kind=kCustom, calls=%fused_computation.110 | custom fusion | bytes 524290 | tf_op jit(solution)/shard_map/scatter | solution.py:112
  126.8 1.6 %fusion.56 = f32[8,128,256]{2,1,0:T(8,128)S(1)} fusion(bf16[256,8,128]{0,2,1:T(8,128)(2,1)} %bitcast.230, bf16[8,256,256]{2,1,0:T(8,128)(2,1)S(1)} %copy-done.7, pred[8]{0:T(512)(128)(4,1)S(1)} %copy-done.55), kind=kOutput, calls=%fused_computation.89 | convolution fusion | flops 134742016 | bytes 2621448 | tf_op jit(solution)/shard_map/toi,itb->otb/dot_general | solution.py:119
  131.3 1.9 %copy.186 = f32[256,4,4,32]{3,2,1,0:T(4,128)} copy(f32[256,4,4,32]{0,3,2,1:T(8,128)S(1)} %pad_maximum_fusion.6) | data formatting | bytes 1048576 | tf_op jit(solution)/shard_map/stack | solution.py:94
  133.2 2.6 %reshape.1295 = f32[4,1,32768]{2,1,0:T(1,128)S(1)} reshape(f32[256,4,4,32]{3,2,1,0:T(4,128)} %copy.186) | data formatting | bytes 1048576
  135.8 11.2 %all_to_all.33 = f32[4,1,32768]{2,1,0:T(1,128)S(1)} all-to-all(f32[4,1,32768]{2,1,0:T(1,128)S(1)} %reshape.1295), channel_id=1, replica_groups=mesh['tile'=8,'trc'=4] {'trc'}, dimensions={0} | all-to-all | bytes 1048576 | tf_op jit(solution)/shard_map/all_to_all | solution.py:177
  147.6 2.1 %reduce.8 = f32[4,32768]{1,0:T(4,128)S(1)} reduce(f32[4,1,32768]{2,1,0:T(1,128)S(1)} %all_to_all.33, f32[]{:T(128)} %broadcast.1161), dimensions={1}, to_apply=%all_to_all.27.reduce_sub_computation | reduce | bytes 1048580 | tf_op jit(solution)/shard_map/all_to_all | solution.py:177
  149.7 2.5 %reshape.1296 = f32[256,4,4,32]{3,2,1,0:T(4,128)} reshape(f32[4,32768]{1,0:T(4,128)S(1)} %reduce.8) | data formatting | bytes 1048576
  152.2 1.9 %copy.188 = f32[64,4,4,4,32]{0,4,3,2,1:T(8,128)S(1)} copy(f32[64,4,4,4,32]{4,2,1,0,3:T(4,128)} %bitcast.224) | data formatting | bytes 1048576 | tf_op jit(solution)/shard_map/all_to_all | solution.py:177
  (253 shorter events, 53.1 us)
Async XLA Ops:
  0.0 35.6 %copy-start = (bf16[4,256,256]{2,1,0:T(8,128)(2,1)S(1)}, bf16[4,256,256]{2,1,0:T(8,128)(2,1)}, u32[]{:S(2)}) copy-start(bf16[4,256,256]{2,1,0:T(8,128)(2,1)} %param.19) | copy-start | bytes 1572868
  0.0 9.0 %copy-start.3 = (f32[64,4,4,128]{3,2,1,0:T(4,128)S(1)}, f32[64,4,4,128]{3,2,1,0:T(4,128)}, u32[]{:S(2)}) copy-start(f32[64,4,4,128]{3,2,1,0:T(4,128)} %param.13) | copy-start | bytes 1572868
  0.0 9.7 %copy-start.22 = (f32[4,4,128]{2,1,0:T(4,128)S(1)}, f32[4,4,128]{2,1,0:T(4,128)}, u32[]{:S(2)}) copy-start(f32[4,4,128]{2,1,0:T(4,128)} %param.14) | copy-start | bytes 24580
  3.0 55.9 %collective-permute-start = (f32[65,4,3,128]{3,1,2,0:T(4,128)}, f32[65,4,3,128]{3,1,2,0:T(4,128)S(1)}, u32[]{:S(2)}, u32[]{:S(2)}) collective-permute-start(f32[65,4,3,128]{3,1,2,0:T(4,128)} %get-tuple-element.46), channel_id=1, source_target_pairs={{4,0},{8,4},{12,8},{16,12},{20,16},{24,20},{28,24},{0,28},{5,1},{9... | collective-permute-start | bytes 1198088 | tf_op jit(solution)/shard_map/ppermute | solution.py:18
  9.0 51.5 %collective-permute-start.1 = (f32[65,4,3,128]{3,1,2,0:T(4,128)}, f32[65,4,3,128]{3,1,2,0:T(4,128)}, u32[]{:S(2)}, u32[]{:S(2)}) collective-permute-start(f32[65,4,3,128]{3,1,2,0:T(4,128)} %get-tuple-element.45), channel_id=1, source_target_pairs={{0,4},{4,8},{8,12},{12,16},{16,20},{20,24},{24,28},{28,0},{1,5},{5... | collective-permute-start | bytes 1198088 | tf_op jit(solution)/shard_map/ppermute | solution.py:15
  22.6 5.3 %copy-start.33 = (s32[4,128]{1,0:T(4,128)S(1)}, s32[4,128]{1,0:T(4,128)}, u32[]{:S(2)}) copy-start(s32[4,128]{1,0:T(4,128)} %eq.156) | copy-start | bytes 6148
  22.6 8.4 %copy-start.14 = (s32[512]{0:T(512)S(1)}, s32[512]{0:T(512)}, u32[]{:S(2)}) copy-start(s32[512]{0:T(512)} %eq.128) | copy-start | bytes 6148
  22.6 8.8 %copy-start.18 = (s32[512]{0:T(512)S(1)}, s32[512]{0:T(512)}, u32[]{:S(2)}) copy-start(s32[512]{0:T(512)} %eq.144) | copy-start | bytes 6148
  22.6 9.1 %copy-start.16 = (s32[512]{0:T(512)S(1)}, s32[512]{0:T(512)}, u32[]{:S(2)}) copy-start(s32[512]{0:T(512)} %eq.136) | copy-start | bytes 6148
  22.6 9.4 %copy-start.58 = (s32[8]{0:T(128)S(1)}, s32[8]{0:T(128)}, u32[]{:S(2)}) copy-start(s32[8]{0:T(128)} %iota_multiply_fusion) | copy-start | bytes 100
  22.6 10.1 %copy-start.32 = (s32[4,128]{1,0:T(4,128)S(1)}, s32[4,128]{1,0:T(4,128)}, u32[]{:S(2)}) copy-start(s32[4,128]{1,0:T(4,128)} %eq.148) | copy-start | bytes 6148
  37.3 6.1 %copy-start.30 = (s32[4,128]{1,0:T(4,128)S(1)}, s32[4,128]{1,0:T(4,128)}, u32[]{:S(2)}) copy-start(s32[4,128]{1,0:T(4,128)} %eq.132) | copy-start | bytes 6148
  41.1 6.2 %copy-start.49 = (s32[4,32]{1,0:T(4,128)S(1)}, s32[4,32]{1,0:T(4,128)}, u32[]{:S(2)}) copy-start(s32[4,32]{1,0:T(4,128)} %param.17) | copy-start | bytes 1540
  41.2 6.8 %copy-start.34 = (f32[3,4,32]{2,1,0:T(4,128)S(1)}, f32[3,4,32]{2,1,0:T(4,128)}, u32[]{:S(2)}) copy-start(f32[3,4,32]{2,1,0:T(4,128)} %param.21) | copy-start | bytes 4612
  45.8 12.0 %copy-start.23 = (s32[512]{0:T(512)}, s32[512]{0:T(512)S(1)}, u32[]{:S(2)}) copy-start(s32[512]{0:T(512)S(1)} %get-tuple-element.30) | copy-start | bytes 6148
  48.1 10.2 %copy-start.35 = (f32[128]{0:T(128)}, f32[128]{0:T(128)S(1)}, u32[]{:S(2)}) copy-start(f32[128]{0:T(128)S(1)} %squeeze.10) | copy-start | bytes 1540
  48.2 10.2 %copy-start.37 = (f32[128]{0:T(128)}, f32[128]{0:T(128)S(1)}, u32[]{:S(2)}) copy-start(f32[128]{0:T(128)S(1)} %squeeze.11) | copy-start | bytes 1540
  48.2 10.1 %copy-start.39 = (f32[128]{0:T(128)}, f32[128]{0:T(128)S(1)}, u32[]{:S(2)}) copy-start(f32[128]{0:T(128)S(1)} %squeeze.9) | copy-start | bytes 1540
  73.2 8.3 %copy-start.2 = (f32[64,4,4,129]{0,2,1,3:T(4,128)S(1)}, f32[64,4,4,129]{0,2,1,3:T(4,128)}, u32[]{:S(2)}) copy-start(f32[64,4,4,129]{0,2,1,3:T(4,128)} %multiply_select_fusion) | copy-start | bytes 1585156
  81.5 5.3 %copy-start.24 = (s32[512]{0:T(512)S(1)}, s32[512]{0:T(512)}, u32[]{:S(2)}) copy-start(s32[512]{0:T(512)} %copy-done.23) | copy-start | bytes 6148
  83.2 9.4 %all-to-all-start = ((bf16[4,2,16384]{2,1,0:T(2,128)(2,1)}), bf16[4,2,16384]{2,1,0:T(2,128)(2,1)S(1)}, u32[]{:S(2)}, u32[]{:S(2)}) async-start(bf16[4,2,16384]{2,1,0:T(2,128)(2,1)} %reshape.1293), calls=%async_computation | async-start | bytes 524288 | tf_op jit(solution)/shard_map/all_to_all | solution.py:167
  93.4 6.7 %copy-start.6 = (bf16[8,256,256]{2,1,0:T(8,128)(2,1)S(1)}, bf16[8,256,256]{2,1,0:T(8,128)(2,1)}, u32[]{:S(2)}) copy-start(bf16[8,256,256]{2,1,0:T(8,128)(2,1)} %gather_fusion) | copy-start | bytes 3145732
  93.4 6.7 %copy-start.54 = (pred[8]{0:T(512)(128)(4,1)S(1)}, pred[8]{0:T(512)(128)(4,1)}, u32[]{:S(2)}) copy-start(pred[8]{0:T(512)(128)(4,1)} %get-tuple-element.71) | copy-start | bytes 28
  101.8 7.2 %copy-start.4 = (bf16[8,256,256]{2,1,0:T(8,128)(2,1)S(1)}, bf16[8,256,256]{2,1,0:T(8,128)(2,1)}, u32[]{:S(2)}) copy-start(bf16[8,256,256]{2,1,0:T(8,128)(2,1)} %gather_fusion.2) | copy-start | bytes 3145732
  101.8 7.2 %copy-start.53 = (pred[8]{0:T(512)(128)(4,1)S(1)}, pred[8]{0:T(512)(128)(4,1)}, u32[]{:S(2)}) copy-start(pred[8]{0:T(512)(128)(4,1)} %get-tuple-element.39) | copy-start | bytes 28
  104.1 6.6 %copy-start.28 = (s32[1024]{0:T(1024)S(1)}, s32[1024]{0:T(1024)}, u32[]{:S(2)}) copy-start(s32[1024]{0:T(1024)} %get-tuple-element.75) | copy-start | bytes 12292
  110.7 7.2 %copy-start.5 = (bf16[8,256,256]{2,1,0:T(8,128)(2,1)S(1)}, bf16[8,256,256]{2,1,0:T(8,128)(2,1)}, u32[]{:S(2)}) copy-start(bf16[8,256,256]{2,1,0:T(8,128)(2,1)} %gather_fusion.4) | copy-start | bytes 3145732
  110.7 7.2 %copy-start.56 = (pred[8]{0:T(512)(128)(4,1)S(1)}, pred[8]{0:T(512)(128)(4,1)}, u32[]{:S(2)}) copy-start(pred[8]{0:T(512)(128)(4,1)} %get-tuple-element.69) | copy-start | bytes 28
  112.9 6.6 %copy-start.27 = (s32[1024]{0:T(1024)S(1)}, s32[1024]{0:T(1024)}, u32[]{:S(2)}) copy-start(s32[1024]{0:T(1024)} %get-tuple-element.74) | copy-start | bytes 12292
  119.5 7.3 %copy-start.7 = (bf16[8,256,256]{2,1,0:T(8,128)(2,1)S(1)}, bf16[8,256,256]{2,1,0:T(8,128)(2,1)}, u32[]{:S(2)}) copy-start(bf16[8,256,256]{2,1,0:T(8,128)(2,1)} %gather_fusion.6) | copy-start | bytes 3145732
  119.5 7.3 %copy-start.55 = (pred[8]{0:T(512)(128)(4,1)S(1)}, pred[8]{0:T(512)(128)(4,1)}, u32[]{:S(2)}) copy-start(pred[8]{0:T(512)(128)(4,1)} %get-tuple-element.31) | copy-start | bytes 28
  122.0 6.4 %copy-start.26 = (s32[1024]{0:T(1024)S(1)}, s32[1024]{0:T(1024)}, u32[]{:S(2)}) copy-start(s32[1024]{0:T(1024)} %get-tuple-element.73) | copy-start | bytes 12292
  (30 other events, 61.9 us)
where the time goes:
time: 157 us; the launch traced here: 155 us
  local copies, waits for them, and re-layouts  70.2 us (45%)
  other arithmetic  44.1 us (28%)
  matrix products  12 us (8%)
  blocking collectives  11.2 us (7%)
  starting transfers between devices  9.61 us (6%)
  waiting for transfers between devices  5.76 us (4%)
  between operations  2.31 us (1%)
    select_n x2, other arithmetic, sweep_flux(): return jnp.where(courant > 0.0, flux_pos, flux_neg)  16.6 us
    scatter x4, local copies, waits for them, and re-layouts, grouped_maps(): jnp.zeros((species, capacity), jnp.bfloat16).at[:, target].set(values)  12.9 us
    all_to_all x1, blocking collectives, shards(): lax.all_to_all(tracer_back, 'trc', split_axis=0, concat_axis=3, tiled=True)  11.2 us
    unnamed x125, local copies, waits for them, and re-layouts  8.77 us
    gather x4, local copies, waits for them, and re-layouts, grouped_maps(): gathered = jnp.take(product.reshape(species, capacity), target, axis=1)  8.54 us
    another operation x12, other arithmetic  6.52 us
    gather x4, local copies, waits for them, and re-layouts, grouped_maps(): chosen = jnp.take(linear_maps, tile_entry, axis=0)  6.42 us
    dot_general x4, matrix products, grouped_maps(): jnp.einsum('toi,itb->otb', chosen, buffer.reshape(species, tile_count, bl...  6.36 us
  transfers between devices with their start and end apart: 3, of which 1 were waited for; matrix products, arithmetic and copies ran while one was open for 32% of the time, Pallas kernels for 0%

commit v1 on v0

v1 whole, which is shorter than its diff:
```python
import functools

import jax
import jax.numpy as jnp
from jax import lax
from jax.experimental import pallas as pl
from jax.experimental.pallas import tpu as pltpu
from jax.sharding import PartitionSpec as P

MESH = pl.DeviceIdType.MESH
WIDTH = 3
CHUNK = 16
f32 = jnp.float32
bf16 = jnp.bfloat16


def block_transpose(parts, lane_block):
    count = len(parts)
    lanes = parts[0].shape[-1]
    step = lanes // count
    parts = list(parts)
    bit = 1
    while bit < count:
        low_half = (lane_block & bit) == 0
        moved = list(parts)
        for i in range(count):
            if i & bit == 0:
                low, high = parts[i], parts[i | bit]
                moved[i] = jnp.where(low_half, low, pltpu.roll(high, step * bit, 1))
                moved[i | bit] = jnp.where(low_half, pltpu.roll(low, lanes - step * bit, 1), high)
        parts = moved
        bit *= 2
    return parts


def flux_weights(u):
    s = jnp.abs(u)
    k = 0.5 * s
    km = k * (1.0 - 2.0 * s / 3.0)
    return u * (1.0 - k - 3.0 * km), u * (k - 3.0 * km), u * (6.0 * km)


def edge_value(a, b, c, d):
    return (7.0 / 12.0) * (b + c) - (1.0 / 12.0) * (a + d)


def kernel(
    dims,
    x_hbm, cc_ref, ce_ref, flag_ref, table_ref, sun_ref, mix_ref, maps_ref, off_ref,
    out_hbm,
    xf, yb, xb, hb, ha, cs, cr, wx, sb, cb, rs, back, mg, offb, coef, mats, load_sem, store_sem,
    halo_send, halo_recv, cour_send, cour_recv, mix_send, mix_recv, fwd_send, fwd_recv, ret_send, ret_recv,
):
    levels, cols, quarter, lanes, tiles, trc, substeps, entries = dims
    me_tile = lax.axis_index("tile")
    me = lax.axis_index("trc")
    after = lax.rem(me_tile + 1, tiles)
    before = lax.rem(me_tile + tiles - 1, tiles)

    loads = []
    for r in range(levels * cols):
        load = pltpu.make_async_copy(x_hbm.at[:, r, 0, :], xf.at[r], load_sem.at[r])
        load.start()
        loads.append(load)

    barrier = pltpu.get_barrier_semaphore()
    for other in (after, before):
        pl.semaphore_signal(barrier, inc=1, device_id={"tile": other, "trc": me}, device_id_type=MESH)
    for d in range(1, trc):
        pl.semaphore_signal(
            barrier, inc=1, device_id={"tile": me_tile, "trc": lax.rem(me + d, trc)}, device_id_type=MESH
        )
    cs[...] = jnp.zeros_like(cs)
    for g in range(levels):
        cs[g : g + 1, :] = cc_ref[g * cols : g * cols + 1, :]
    pl.semaphore_wait(barrier, 2 + trc - 1)

    cour = pltpu.make_async_remote_copy(
        src_ref=cs, dst_ref=cr, send_sem=cour_send, recv_sem=cour_recv,
        device_id={"tile": before, "trc": me}, device_id_type=MESH,
    )
    cour.start()

    halos = []
    for g in range(levels):
        for c in range(cols):
            loads[g * cols + c].wait()
            xb[g, c] = xf[g * cols + c].astype(bf16)
        pair = []
        for way, (other, first, dst) in enumerate(((after, cols - WIDTH, hb), (before, 0, ha))):
            copy = pltpu.make_async_remote_copy(
                src_ref=xb.at[g, pl.ds(first, WIDTH)], dst_ref=dst.at[g],
                send_sem=halo_send.at[way, g], recv_sem=halo_recv.at[way, g],
                device_id={"tile": other, "trc": me}, device_id_type=MESH,
            )
            copy.start()
            pair.append(copy)
        halos.append(pair)
    mixes = []
    for d in range(1, trc):
        copy = pltpu.make_async_remote_copy(
            src_ref=mix_ref, dst_ref=mg.at[me], send_sem=mix_send.at[d - 1], recv_sem=mix_recv.at[d - 1],
            device_id={"tile": me_tile, "trc": lax.rem(me + d, trc)}, device_id_type=MESH,
        )
        copy.start()
        mixes.append(copy)
    mg[me] = mix_ref[...]

    lane = lax.broadcasted_iota(jnp.int32, (CHUNK, lanes), 1)
    lane_block = lane // (lanes // trc)
    u_edge = ce_ref[...]
    row_lane = lax.broadcasted_iota(jnp.int32, u_edge.shape, 1)
    u_edge = jnp.where(row_lane == 0, 0.0, u_edge)
    wa, wb, wc = flux_weights(u_edge)
    wx[0], wx[1], wx[2], wx[3] = wa, wb, wc, u_edge
    chunks = quarter // CHUNK

    def edge_row(r, _):
        a_w = wx[0, pl.ds(r, 1), :]
        b_w = wx[1, pl.ds(r, 1), :]
        c_w = wx[2, pl.ds(r, 1), :]
        up = jnp.broadcast_to(wx[3, pl.ds(r, 1), :], (CHUNK, lanes)) > 0.0
        for i in range(chunks):
            cell = xf[r, pl.ds(i * CHUNK, CHUNK), :]
            m1 = jnp.where(lane < 1, cell, pltpu.roll(cell, 1, 1))
            m2 = jnp.where(lane < 1, cell, pltpu.roll(m1, 1, 1))
            p1 = jnp.where(lane == lanes - 1, cell, pltpu.roll(cell, lanes - 1, 1))
            a = edge_value(m2, m1, cell, p1)
            a_low = pltpu.roll(a, 1, 1)
            last = edge_value(m1, cell, cell, cell)
            a_high = jnp.where(lane == lanes - 1, last, pltpu.roll(a, lanes - 1, 1))
            flux = a_w * a + b_w * jnp.where(up, a_low, a_high) + c_w * jnp.where(up, m1, cell)
            yb[r, pl.ds(i * CHUNK, CHUNK), :] = cell + (flux - pltpu.roll(flux, lanes - 1, 1))
        return 0

    lax.fori_loop(0, levels * cols, edge_row, 0)

    for e in range(entries):
        offb[e] = jnp.broadcast_to(off_ref[:, e : e + 1], offb.shape[1:])
    src = lax.broadcasted_iota(jnp.int32, (lanes, lanes), 0)
    dst = lax.broadcasted_iota(jnp.int32, (lanes, lanes), 1)
    for side in range(2):
        target = jnp.where(flag_ref[0, side] > 0, lanes - 1 - src, src)
        mats[side] = jnp.where(target == dst, 1.0, 0.0)

    cour.wait()
    u_after = jnp.dot(cr[...], mats[1], precision=lax.Precision.HIGHEST, preferred_element_type=f32)
    for g in range(levels):
        coef[3, g] = jnp.zeros(coef.shape[2:], f32)
        coef[3, g, 0:cols, :] = cc_ref[g * cols : (g + 1) * cols, :]
        coef[3, g, cols : cols + 1, :] = u_after[g : g + 1, :]
    wa, wb, wc = flux_weights(coef[3])
    coef[0], coef[1], coef[2] = wa, wb, wc
    rev = [mats[side].astype(bf16) for side in range(2)]

    def cycle_level(g):
        for copy in halos[g]:
            copy.wait_recv()
        ups = [jnp.broadcast_to(coef[3, g, f : f + 1, :], (CHUNK, lanes)) > 0.0 for f in range(cols + 1)]

        def chunk(i, _):
            rows = pl.ds(pl.multiple_of(i * CHUNK, CHUNK), CHUNK)
            cells = [jnp.dot(hb[g, k, rows, :], rev[0], preferred_element_type=f32) for k in range(WIDTH)]
            cells += [xf[g * cols + c, rows, :] for c in range(cols)]
            cells += [jnp.dot(ha[g, k, rows, :], rev[1], preferred_element_type=f32) for k in range(WIDTH)]
            edges = [edge_value(*cells[k : k + 4]) for k in range(cols + 3)]
            fluxes = []
            for f in range(cols + 1):
                far = jnp.where(ups[f], edges[f], edges[f + 2])
                q = jnp.where(ups[f], cells[f + 2], cells[f + 3])
                fluxes.append(
                    coef[0, g, f : f + 1, :] * edges[f + 1]
                    + coef[1, g, f : f + 1, :] * far
                    + coef[2, g, f : f + 1, :] * q
                )
            moved = [yb[g * cols + c, rows, :] + (fluxes[c] - fluxes[c + 1]) for c in range(cols)]
            moved = block_transpose(moved, lane_block)
            for p in range(trc):
                sb[g, p, rows, :] = moved[p].astype(bf16)
            return 0

        lax.fori_loop(0, chunks, chunk, 0)
        sends = []
        for d in range(1, trc):
            peer = lax.rem(me + d, trc)
            copy = pltpu.make_async_remote_copy(
                src_ref=sb.at[g, peer], dst_ref=cb.at[g, me],
                send_sem=fwd_send.at[d - 1, g], recv_sem=fwd_recv.at[d - 1, g],
                device_id={"tile": me_tile, "trc": peer}, device_id_type=MESH,
            )
            copy.start()
            sends.append(copy)
        cb[g, me] = sb[g, me]
        return sends

    species = quarter * trc
    sun = jnp.broadcast_to(sun_ref[...], (species, lanes)) > 0

    def chem_level(g, sends):
        for copy in sends:
            copy.wait_recv()
        conc = cb[g].reshape(species, lanes)
        state = conc
        for s in range(substeps):
            product = jnp.dot(maps_ref[...], state, preferred_element_type=f32)
            entry = jnp.broadcast_to(table_ref[s * levels + g : s * levels + g + 1, :], (species, lanes))
            result = product[:species] + offb[0]
            for e in range(1, entries):
                result = jnp.where(entry == e, product[e * species : (e + 1) * species] + offb[e], result)
            result = jnp.maximum(result, 0.0)
            state = result.astype(bf16)
        chem = jnp.where(sun, result, conc.astype(f32)).astype(bf16)
        rs[g] = chem.reshape(trc, quarter, lanes)
        copies = []
        for d in range(1, trc):
            peer = lax.rem(me + d, trc)
            copy = pltpu.make_async_remote_copy(
                src_ref=rs.at[g, peer], dst_ref=back.at[g, me],
                send_sem=ret_send.at[d - 1, g], recv_sem=ret_recv.at[d - 1, g],
                device_id={"tile": me_tile, "trc": peer}, device_id_type=MESH,
            )
            copy.start()
            copies.append(copy)
        back[g, me] = rs[g, me]
        return copies

    sends = []
    returns = []
    for g in range(levels):
        sends.append(cycle_level(g))
        if g > 0:
            returns.append(chem_level(g - 1, sends[g - 1]))
    returns.append(chem_level(levels - 1, sends[levels - 1]))

    for copy in mixes:
        copy.wait()
    small_block = lax.broadcasted_iota(jnp.int32, mg.shape[1:], 1) // (lanes // trc)
    mixing = block_transpose([mg[q] for q in range(trc)], small_block)
    inverse, below, ratio = [], [], []
    for c in range(cols):
        k = [mixing[c][l : l + 1, :] for l in range(levels - 1)]
        inv_c, rat_c = [], []
        for l in range(levels):
            k_low = k[l - 1] if l > 0 else None
            k_high = k[l] if l < levels - 1 else None
            pivot = 1.0
            if k_low is not None:
                pivot = pivot + k_low - k_low * rat_c[-1]
            if k_high is not None:
                pivot = pivot + k_high
            inv = 1.0 / pivot
            inv_c.append(inv)
            rat_c.append(k_high * inv if k_high is not None else None)
        inverse.append(inv_c)
        ratio.append(rat_c)
        below.append(k)

    for pair in returns:
        for copy in pair:
            copy.wait_recv()

    def solve_chunk(i, _):
        rows = pl.ds(pl.multiple_of(i * CHUNK, CHUNK), CHUNK)
        chem = []
        for g in range(levels):
            chem.append(block_transpose([back[g, q, rows, :].astype(f32) for q in range(trc)], lane_block))
        for c in range(cols):
            solved = []
            for l in range(levels):
                value = chem[l][c]
                if l > 0:
                    value = value + below[c][l - 1] * solved[-1]
                solved.append(value * inverse[c][l])
            current = solved[-1]
            xf[(levels - 1) * cols + c, rows, :] = current
            for l in range(levels - 2, -1, -1):
                current = solved[l] + ratio[c][l] * current
                xf[l * cols + c, rows, :] = current
        return 0

    lax.fori_loop(0, chunks, solve_chunk, 0)
    stores = []
    for r in range(levels * cols):
        store = pltpu.make_async_copy(xf.at[r], out_hbm.at[:, r, 0, :], store_sem.at[r])
        store.start()
        stores.append(store)
    for group in halos + sends + returns:
        for copy in group:
            copy.wait_send()
    for store in stores:
        store.wait()


def shards(
    tiles, trc,
    tracers, courant_cycle, courant_edge, seam_flags, sunlit, table_entry, linear_maps, offsets, mixing,
):
    quarter, levels, cols, lanes = tracers.shape
    substeps = table_entry.shape[0]
    entries, species, _ = linear_maps.shape
    rows = levels * cols
    dims = (levels, cols, quarter, lanes, tiles, trc, substeps, entries)
    vmem = pl.BlockSpec(memory_space=pltpu.VMEM)
    hbm = pl.BlockSpec(memory_space=pl.ANY)
    smem = pl.BlockSpec(memory_space=pltpu.SMEM)
    dma = pltpu.SemaphoreType.DMA
    mix = jnp.pad(mixing.reshape(levels - 1, lanes), ((0, 8 - (levels - 1)), (0, 0)))
    out = pl.pallas_call(
        functools.partial(kernel, dims),
        out_shape=jax.ShapeDtypeStruct((quarter, rows, 1, lanes), f32),
        in_specs=[hbm, vmem, vmem, smem, vmem, vmem, vmem, vmem, vmem],
        out_specs=hbm,
        scratch_shapes=[
            pltpu.VMEM((rows, quarter, lanes), f32),
            pltpu.VMEM((rows, quarter, lanes), f32),
            pltpu.VMEM((levels, cols, quarter, lanes), bf16),
            pltpu.VMEM((levels, WIDTH, quarter, lanes), bf16),
            pltpu.VMEM((levels, WIDTH, quarter, lanes), bf16),
            pltpu.VMEM((8, lanes), f32),
            pltpu.VMEM((8, lanes), f32),
            pltpu.VMEM((4, rows, lanes), f32),
            pltpu.VMEM((levels, trc, quarter, lanes), bf16),
            pltpu.VMEM((levels, trc, quarter, lanes), bf16),
            pltpu.VMEM((levels, trc, quarter, lanes), bf16),
            pltpu.VMEM((levels, trc, quarter, lanes), bf16),
            pltpu.VMEM((trc, 8, lanes), f32),
            pltpu.VMEM((entries, species, lanes), f32),
            pltpu.VMEM((4, levels, 8, lanes), f32),
            pltpu.VMEM((2, lanes, lanes), f32),
            dma((rows,)),
            dma((rows,)),
            dma((2, levels)),
            dma((2, levels)),
            dma,
            dma,
            dma((trc - 1,)),
            dma((trc - 1,)),
            dma((trc - 1, levels)),
            dma((trc - 1, levels)),
            dma((trc - 1, levels)),
            dma((trc - 1, levels)),
        ],
        compiler_params=pltpu.CompilerParams(
            collective_id=0, has_side_effects=True, vmem_limit_bytes=40 * 1024 * 1024
        ),
    )(
        tracers.reshape(quarter, rows, 1, lanes),
        courant_cycle.reshape(rows, lanes),
        courant_edge.reshape(rows, lanes),
        seam_flags,
        table_entry.reshape(substeps * levels, lanes),
        sunlit.reshape(1, lanes),
        mix,
        linear_maps.reshape(entries * species, species),
        offsets.T,
    )
    return out.reshape(tracers.shape)


def solution(mesh):
    placed = (
        P("trc", None, "tile", None),
        P(None, "tile", None),
        P(None, "tile", None),
        P("tile", None),
        P("tile", "trc"),
        P(None, None, "tile", "trc"),
        P(),
        P(),
        P(None, "tile", "trc"),
    )
    return jax.shard_map(
        functools.partial(shards, mesh.shape["tile"], mesh.shape["trc"]),
        mesh=mesh, in_specs=placed, out_specs=P("trc", None, "tile", None), check_vma=False,
    )
```

time: 157 us -> 37.6 us (0.24)
  local copies, waits for them, and re-layouts: 70.2 us -> 5.4 us
  other arithmetic: 44.1 us -> 0 us
  Pallas kernels: 0 us -> 31.8 us
  matrix products: 12 us -> 0 us
  blocking collectives: 11.2 us -> 0 us
  starting transfers between devices: 9.61 us -> 0 us
  waiting for transfers between devices: 5.76 us -> 0 us
  between operations: 2.31 us -> 0.04 us
    pallas_call x0 -> x1, Pallas kernels: none -> 31.8 us  [shards(): pl.pallas_call(functools.partial(kernel, dims), out_shape=jax.ShapeDtypeS...]
    select_n x13 -> x0, other arithmetic: 19.7 us -> none  [the longest x2 16.6 us: sweep_flux(): return jnp.where(courant > 0.0, flux_pos, flux_neg)]
    gather x8 -> x0, local copies, waits for them, and re-layouts: 15 us -> none  [the longest x4 8.54 us: grouped_maps(): gathered = jnp.take(product.reshape(species, capacity), target, axis=1)]
    scatter x4 -> x0, local copies, waits for them, and re-layouts: 12.9 us -> none  [grouped_maps(): jnp.zeros((species, capacity), jnp.bfloat16).at[:, target].set(values)]
    dot_general x8 -> x0, matrix products: 12 us -> none  [the longest x4 6.36 us: grouped_maps(): jnp.einsum('toi,itb->otb', chosen, buffer.reshape(species, tile_count, bl...]
    all_to_all x1 -> x0, blocking collectives: 11.2 us -> none  [shards(): lax.all_to_all(tracer_back, 'trc', split_axis=0, concat_axis=3, tiled=True)]
    slice x12 -> x0, local copies, waits for them, and re-layouts: 6.94 us -> none  [the longest x1 1.42 us: shards(): before[:quarter]]
    another operation x13 -> x0, other arithmetic: 6.56 us -> none
  transfers between devices with their start and end apart: 3 -> 0, of which waited for: 1 -> 0; matrix products, arithmetic and copies ran while one was open for 32% -> 0% of each run, Pallas kernels for 0% -> 0%
where the time goes in v1:
time: 37.6 us; the launch traced here: 37.2 us
  Pallas kernels  31.8 us (85%)
  local copies, waits for them, and re-layouts  5.4 us (14%)
    pallas_call x1, Pallas kernels, shards(): pl.pallas_call(functools.partial(kernel, dims), out_shape=jax.ShapeDtypeS...  31.8 us
    unnamed x16, local copies, waits for them, and re-layouts  3.68 us
    reshape x1, local copies, waits for them, and re-layouts, shards(): table_entry.reshape(substeps * levels, lanes)  0.86 us
    reshape x1, local copies, waits for them, and re-layouts, shards(): sunlit.reshape(1, lanes)  0.78 us

profile of v1, /device:TPU:0, one launch (start us, length us, event | category | flops | bytes accessed | tf_op | source)
XLA Modules:
  0.0 37.2 jit_solution(4098640039260753724)
XLA Ops:
  0.0 0.0 copy-start.5
  0.0 0.8 %reshape.28.sun_ref = s32[1,128]{1,0:T(1,128)S(1)} reshape(s32[4,32]{1,0:T(4,128)} %param.13) | data formatting | bytes 1024 | tf_op jit(solution)/shard_map/reshape | solution.py:352
  0.8 0.0 copy-done.5
  0.8 0.1 reshape.29
  0.9 0.0 copy-start.6
  0.9 0.9 %reshape.27.table_ref = s32[16,128]{1,0:T(8,128)S(1)} reshape(s32[4,4,4,32]{3,2,1,0:T(4,128)} %param.14) | data formatting | bytes 16384 | tf_op jit(solution)/shard_map/reshape | solution.py:351
  1.7 0.0 copy-done.6
  1.7 0.0 copy-start.2
  1.7 0.0 copy-start.3
  1.8 0.1 copy.10
  1.9 0.0 copy-start.4
  1.9 0.5 %copy-done.2 = f32[4,4,128]{2,1,0:T(4,128)S(1)} copy-done((f32[4,4,128]{2,1,0:T(4,128)S(1)}, f32[4,4,128]{2,1,0:T(4,128)}, u32[]{:S(2)}) %copy-start.2) | copy-done | bytes 8216
  2.4 0.0 copy-done.3
  2.5 0.1 copy-done.4
  2.6 0.0 copy-start
  2.6 1.0 %copy-done = f32[64,4,4,128]{3,2,1,0:T(4,128)S(1)} copy-done((f32[64,4,4,128]{3,2,1,0:T(4,128)S(1)}, f32[64,4,4,128]{3,2,1,0:T(4,128)}, u32[]{:S(2)}) %copy-start) | copy-done | bytes 524312
  3.6 0.0 copy-start.1
  3.6 1.0 %copy-done.1 = bf16[4,256,256]{2,1,0:T(8,128)(2,1)S(1)} copy-done((bf16[4,256,256]{2,1,0:T(8,128)(2,1)S(1)}, bf16[4,256,256]{2,1,0:T(8,128)(2,1)}, u32[]{:S(2)}) %copy-start.1) | copy-done | bytes 524312
  4.6 31.8 %shard_map.91 = f32[64,16,1,128]{3,2,1,0:T(1,128)S(1)} custom-call(f32[64,16,1,128]{3,2,1,0:T(1,128)S(1)} %bitcast.7, f32[16,128]{1,0:T(8,128)S(1)} %bitcast.10, f32[16,128]{1,0:T(8,128)S(1)} %bitcast.11, s32[1,2]{1,0:T(1,128)S(1)} %copy-done.4, s32[16,128]{1,0:T(8,128)S(1)} %reshape.27.table_ref, s32[1,128]{1,0:T(1,128)S(1)} %reshape.28.sun_ref, ...), custom_call_target="tpu_custom_call" | custom-call | tf_op jit(solution)/shard_map/pallas_call | solution.py:308
  36.4 0.8 %copy.12 = f32[64,4,4,128]{3,2,1,0:T(4,128)} copy(f32[64,4,4,128]{3,2,1,0:T(4,128)S(1)} %bitcast.6) | data formatting | bytes 1048576
  (1 shorter events, 0.0 us)
Async XLA Ops:
  0.0 0.8 %copy-start.5 = (f32[3,4,32]{2,1,0:T(4,128)S(1)}, f32[3,4,32]{2,1,0:T(4,128)}, u32[]{:S(2)}) copy-start(f32[3,4,32]{2,1,0:T(4,128)} %param.17) | copy-start | bytes 4612
  0.9 0.9 %copy-start.6 = (f32[4,256]{1,0:T(4,128)S(1)}, f32[4,256]{1,0:T(4,128)}, u32[]{:S(2)}) copy-start(f32[4,256]{1,0:T(4,128)} %param.16) | copy-start | bytes 12292
  1.7 0.7 %copy-start.2 = (f32[4,4,128]{2,1,0:T(4,128)S(1)}, f32[4,4,128]{2,1,0:T(4,128)}, u32[]{:S(2)}) copy-start(f32[4,4,128]{2,1,0:T(4,128)} %param.10) | copy-start | bytes 24580
  1.7 0.7 %copy-start.3 = (f32[4,4,128]{2,1,0:T(4,128)S(1)}, f32[4,4,128]{2,1,0:T(4,128)}, u32[]{:S(2)}) copy-start(f32[4,4,128]{2,1,0:T(4,128)} %param.11) | copy-start | bytes 24580
  1.9 0.7 %copy-start.4 = (s32[1,2]{1,0:T(1,128)S(1)}, s32[1,2]{1,0:T(1,128)}, u32[]{:S(2)}) copy-start(s32[1,2]{1,0:T(1,128)} %flag_ref.1) | copy-start | bytes 28
  2.6 1.0 %copy-start = (f32[64,4,4,128]{3,2,1,0:T(4,128)S(1)}, f32[64,4,4,128]{3,2,1,0:T(4,128)}, u32[]{:S(2)}) copy-start(f32[64,4,4,128]{3,2,1,0:T(4,128)} %param.9) | copy-start | bytes 1572868
  3.6 1.0 %copy-start.1 = (bf16[4,256,256]{2,1,0:T(8,128)(2,1)S(1)}, bf16[4,256,256]{2,1,0:T(8,128)(2,1)}, u32[]{:S(2)}) copy-start(bf16[4,256,256]{2,1,0:T(8,128)(2,1)} %param.15) | copy-start | bytes 1572868

commit v2 on v1

--- a/solution.py
+++ b/solution.py
@@ -46,9 +46,10 @@
 
 def kernel(
     dims,
-    x_hbm, cc_ref, ce_ref, flag_ref, table_ref, sun_ref, mix_ref, maps_ref, off_ref,
+    x_hbm, cc_hbm, ce_hbm, flag_ref, table_hbm, sun_hbm, mix_hbm, maps_hbm, off_hbm,
     out_hbm,
-    xf, yb, xb, hb, ha, cs, cr, wx, sb, cb, rs, back, mg, offb, coef, mats, load_sem, store_sem,
+    xf, yb, xb, hb, ha, cs, cr, wx, sb, cb, rs, back, mg, offb, coef, mats,
+    cc_ref, ce_ref, tv, sv, mv, maps_ref, off_ref, table_ref, sun_ref, mix_ref, small_sem, load_sem, store_sem,
     halo_send, halo_recv, cour_send, cour_recv, mix_send, mix_recv, fwd_send, fwd_recv, ret_send, ret_recv,
 ):
     levels, cols, quarter, lanes, tiles, trc, substeps, entries = dims
@@ -57,11 +58,21 @@
     after = lax.rem(me_tile + 1, tiles)
     before = lax.rem(me_tile + tiles - 1, tiles)
 
+    first = pltpu.make_async_copy(cc_hbm, cc_ref, small_sem.at[0])
+    first.start()
     loads = []
     for r in range(levels * cols):
         load = pltpu.make_async_copy(x_hbm.at[:, r, 0, :], xf.at[r], load_sem.at[r])
         load.start()
         loads.append(load)
+
+    smalls = []
+    for i, (source, target) in enumerate(
+        ((mix_hbm, mv), (ce_hbm, ce_ref), (off_hbm, off_ref), (sun_hbm, sv), (table_hbm, tv), (maps_hbm, maps_ref))
+    ):
+        load = pltpu.make_async_copy(source, target, small_sem.at[i + 1])
+        load.start()
+        smalls.append(load)
 
     barrier = pltpu.get_barrier_semaphore()
     for other in (after, before):
@@ -70,6 +81,7 @@
         pl.semaphore_signal(
             barrier, inc=1, device_id={"tile": me_tile, "trc": lax.rem(me + d, trc)}, device_id_type=MESH
         )
+    first.wait()
     cs[...] = jnp.zeros_like(cs)
     for g in range(levels):
         cs[g : g + 1, :] = cc_ref[g * cols : g * cols + 1, :]
@@ -96,6 +108,12 @@
             copy.start()
             pair.append(copy)
         halos.append(pair)
+    for load in smalls:
+        load.wait()
+    mix_ref[...] = jnp.zeros_like(mix_ref)
+    mix_ref[0 : levels - 1, :] = jnp.concatenate([mv[:, c, :] for c in range(cols)], axis=1)
+    table_ref[...] = jnp.concatenate([tv[:, c, :] for c in range(cols)], axis=1)
+    sun_ref[...] = jnp.concatenate([sv[c : c + 1, :] for c in range(cols)], axis=1)
     mixes = []
     for d in range(1, trc):
         copy = pltpu.make_async_remote_copy(
@@ -136,7 +154,11 @@
     lax.fori_loop(0, levels * cols, edge_row, 0)
 
     for e in range(entries):
-        offb[e] = jnp.broadcast_to(off_ref[:, e : e + 1], offb.shape[1:])
+        picked = lax.broadcasted_iota(jnp.int32, (entries, lanes), 0) == e
+        offb[e] = lax.dot_general(
+            off_ref[...], jnp.where(picked, 1.0, 0.0), (((0,), (0,)), ((), ())),
+            precision=lax.Precision.HIGHEST, preferred_element_type=f32,
+        )
     src = lax.broadcasted_iota(jnp.int32, (lanes, lanes), 0)
     dst = lax.broadcasted_iota(jnp.int32, (lanes, lanes), 1)
     for side in range(2):
@@ -300,15 +322,13 @@
     entries, species, _ = linear_maps.shape
     rows = levels * cols
     dims = (levels, cols, quarter, lanes, tiles, trc, substeps, entries)
-    vmem = pl.BlockSpec(memory_space=pltpu.VMEM)
     hbm = pl.BlockSpec(memory_space=pl.ANY)
     smem = pl.BlockSpec(memory_space=pltpu.SMEM)
     dma = pltpu.SemaphoreType.DMA
-    mix = jnp.pad(mixing.reshape(levels - 1, lanes), ((0, 8 - (levels - 1)), (0, 0)))
     out = pl.pallas_call(
         functools.partial(kernel, dims),
         out_shape=jax.ShapeDtypeStruct((quarter, rows, 1, lanes), f32),
-        in_specs=[hbm, vmem, vmem, smem, vmem, vmem, vmem, vmem, vmem],
+        in_specs=[hbm, hbm, hbm, smem, hbm, hbm, hbm, hbm, hbm],
         out_specs=hbm,
         scratch_shapes=[
             pltpu.VMEM((rows, quarter, lanes), f32),
@@ -327,6 +347,17 @@
             pltpu.VMEM((entries, species, lanes), f32),
             pltpu.VMEM((4, levels, 8, lanes), f32),
             pltpu.VMEM((2, lanes, lanes), f32),
+            pltpu.VMEM((rows, lanes), f32),
+            pltpu.VMEM((rows, lanes), f32),
+            pltpu.VMEM((substeps * levels, cols, lanes // trc), jnp.int32),
+            pltpu.VMEM((cols, lanes // trc), jnp.int32),
+            pltpu.VMEM((levels - 1, cols, lanes // trc), f32),
+            pltpu.VMEM((entries * species, species), bf16),
+            pltpu.VMEM((entries, species), f32),
+            pltpu.VMEM((substeps * levels, lanes), jnp.int32),
+            pltpu.VMEM((1, lanes), jnp.int32),
+            pltpu.VMEM((8, lanes), f32),
+            dma((7,)),
             dma((rows,)),
             dma((rows,)),
             dma((2, levels)),
@@ -341,18 +372,18 @@
             dma((trc - 1, levels)),
         ],
         compiler_params=pltpu.CompilerParams(
-            collective_id=0, has_side_effects=True, vmem_limit_bytes=40 * 1024 * 1024
+            collective_id=0, has_side_effects=True, vmem_limit_bytes=60 * 1024 * 1024
         ),
     )(
         tracers.reshape(quarter, rows, 1, lanes),
         courant_cycle.reshape(rows, lanes),
         courant_edge.reshape(rows, lanes),
         seam_flags,
-        table_entry.reshape(substeps * levels, lanes),
-        sunlit.reshape(1, lanes),
-        mix,
+        table_entry.reshape(substeps * levels, cols, lanes // trc),
+        sunlit,
+        mixing,
         linear_maps.reshape(entries * species, species),
-        offsets.T,
+        offsets,
     )
     return out.reshape(tracers.shape)
 

time: 37.6 us -> 34.6 us (0.920)
  local copies, waits for them, and re-layouts: 5.4 us -> 1.87 us
  Pallas kernels: 31.8 us -> 32.6 us
    unnamed x16 -> x1, local copies, waits for them, and re-layouts: 3.68 us -> 1.87 us
    reshape x3 -> x0, local copies, waits for them, and re-layouts: 1.71 us -> none  [the longest x1 0.86 us: shards(): table_entry.reshape(substeps * levels, lanes)]
    pallas_call x1, Pallas kernels: 31.8 us -> 32.6 us  [shards(): pl.pallas_call(functools.partial(kernel, dims), out_shape=jax.ShapeDtypeS...]
where the time goes in v2:
time: 34.6 us; the launch traced here: 34.4 us
  Pallas kernels  32.6 us (94%)
  local copies, waits for them, and re-layouts  1.87 us (5%)
    pallas_call x1, Pallas kernels, shards(): pl.pallas_call(functools.partial(kernel, dims), out_shape=jax.ShapeDtypeS...  32.6 us
    unnamed x1, local copies, waits for them, and re-layouts  1.87 us

profile of v2, /device:TPU:0, one launch (start us, length us, event | category | flops | bytes accessed | tf_op | source)
XLA Modules:
  0.0 34.4 jit_solution(602041695352379262)
XLA Ops:
  0.0 32.6 %shard_map.91 = f32[64,16,1,128]{3,2,1,0:T(1,128)} custom-call(f32[64,16,1,128]{3,2,1,0:T(1,128)} %bitcast.7, f32[16,128]{1,0:T(8,128)} %bitcast.10, f32[16,128]{1,0:T(8,128)} %bitcast.11, s32[1,2]{1,0:T(1,128)} %flag_ref.1, s32[16,4,32]{2,1,0:T(4,128)} %bitcast.9, s32[4,32]{1,0:T(4,128)} %sun_hbm.1, f32[3,4,32]{2,1,0:T(4,128)} %mix_hbm.1, ...), custom_call_target="tpu_custom_call" | custom-call | tf_op jit(solution)/shard_map/pallas_call | solution.py:328
  32.6 1.9 %copy.11 = f32[64,4,4,128]{3,2,1,0:T(4,128)} copy(f32[64,4,4,128]{3,2,1,0:T(4,128)} %bitcast.6) | data formatting | bytes 1048576

commit v3 on v2

--- a/solution.py
+++ b/solution.py
@@ -48,7 +48,7 @@
     dims,
     x_hbm, cc_hbm, ce_hbm, flag_ref, table_hbm, sun_hbm, mix_hbm, maps_hbm, off_hbm,
     out_hbm,
-    xf, yb, xb, hb, ha, cs, cr, wx, sb, cb, rs, back, mg, offb, coef, mats,
+    xf, yb, xb, hb, ha, cs, cr, wx, sb, cb, rs, back, mg, offb, coef, mats, hf,
     cc_ref, ce_ref, tv, sv, mv, maps_ref, off_ref, table_ref, sun_ref, mix_ref, small_sem, load_sem, store_sem,
     halo_send, halo_recv, cour_send, cour_recv, mix_send, mix_recv, fwd_send, fwd_recv, ret_send, ret_recv,
 ):
@@ -141,17 +141,19 @@
         for i in range(chunks):
             cell = xf[r, pl.ds(i * CHUNK, CHUNK), :]
             m1 = jnp.where(lane < 1, cell, pltpu.roll(cell, 1, 1))
-            m2 = jnp.where(lane < 1, cell, pltpu.roll(m1, 1, 1))
+            m2 = jnp.where(lane < 2, m1, pltpu.roll(cell, 2, 1))
+            m3 = jnp.where(lane < 3, m2, pltpu.roll(cell, 3, 1))
             p1 = jnp.where(lane == lanes - 1, cell, pltpu.roll(cell, lanes - 1, 1))
-            a = edge_value(m2, m1, cell, p1)
-            a_low = pltpu.roll(a, 1, 1)
-            last = edge_value(m1, cell, cell, cell)
-            a_high = jnp.where(lane == lanes - 1, last, pltpu.roll(a, lanes - 1, 1))
-            flux = a_w * a + b_w * jnp.where(up, a_low, a_high) + c_w * jnp.where(up, m1, cell)
+            p2 = jnp.where(lane >= lanes - 2, p1, pltpu.roll(cell, lanes - 2, 1))
+            near = edge_value(m2, m1, cell, p1)
+            far = edge_value(
+                jnp.where(up, m3, m1), jnp.where(up, m2, cell), jnp.where(up, m1, p1), jnp.where(up, cell, p2)
+            )
+            flux = a_w * near + b_w * far + c_w * jnp.where(up, m1, cell)
             yb[r, pl.ds(i * CHUNK, CHUNK), :] = cell + (flux - pltpu.roll(flux, lanes - 1, 1))
         return 0
 
-    lax.fori_loop(0, levels * cols, edge_row, 0)
+    lax.fori_loop(0, levels * cols, edge_row, 0, unroll=2)
 
     for e in range(entries):
         picked = lax.broadcasted_iota(jnp.int32, (entries, lanes), 0) == e
@@ -178,13 +180,16 @@
     def cycle_level(g):
         for copy in halos[g]:
             copy.wait_recv()
+        for side, halo in enumerate((hb, ha)):
+            turned = jnp.dot(halo[g].reshape(WIDTH * quarter, lanes), rev[side], preferred_element_type=f32)
+            hf[side] = turned.reshape(WIDTH, quarter, lanes)
         ups = [jnp.broadcast_to(coef[3, g, f : f + 1, :], (CHUNK, lanes)) > 0.0 for f in range(cols + 1)]
 
         def chunk(i, _):
             rows = pl.ds(pl.multiple_of(i * CHUNK, CHUNK), CHUNK)
-            cells = [jnp.dot(hb[g, k, rows, :], rev[0], preferred_element_type=f32) for k in range(WIDTH)]
+            cells = [hf[0, k, rows, :] for k in range(WIDTH)]
             cells += [xf[g * cols + c, rows, :] for c in range(cols)]
-            cells += [jnp.dot(ha[g, k, rows, :], rev[1], preferred_element_type=f32) for k in range(WIDTH)]
+            cells += [hf[1, k, rows, :] for k in range(WIDTH)]
             edges = [edge_value(*cells[k : k + 4]) for k in range(cols + 3)]
             fluxes = []
             for f in range(cols + 1):
@@ -201,7 +206,7 @@
                 sb[g, p, rows, :] = moved[p].astype(bf16)
             return 0
 
-        lax.fori_loop(0, chunks, chunk, 0)
+        lax.fori_loop(0, chunks, chunk, 0, unroll=2)
         sends = []
         for d in range(1, trc):
             peer = lax.rem(me + d, trc)
@@ -218,41 +223,42 @@
     species = quarter * trc
     sun = jnp.broadcast_to(sun_ref[...], (species, lanes)) > 0
 
-    def chem_level(g, sends):
-        for copy in sends:
-            copy.wait_recv()
-        conc = cb[g].reshape(species, lanes)
-        state = conc
+    def chem_levels(group):
+        for g in group:
+            for copy in sends[g]:
+                copy.wait_recv()
+        conc = [cb[g].reshape(species, lanes) for g in group]
+        states = conc
         for s in range(substeps):
-            product = jnp.dot(maps_ref[...], state, preferred_element_type=f32)
-            entry = jnp.broadcast_to(table_ref[s * levels + g : s * levels + g + 1, :], (species, lanes))
-            result = product[:species] + offb[0]
-            for e in range(1, entries):
-                result = jnp.where(entry == e, product[e * species : (e + 1) * species] + offb[e], result)
-            result = jnp.maximum(result, 0.0)
-            state = result.astype(bf16)
-        chem = jnp.where(sun, result, conc.astype(f32)).astype(bf16)
-        rs[g] = chem.reshape(trc, quarter, lanes)
+            product = jnp.dot(maps_ref[...], jnp.concatenate(states, axis=1), preferred_element_type=f32)
+            results = []
+            for i, g in enumerate(group):
+                row = s * levels + g
+                entry = jnp.broadcast_to(table_ref[row : row + 1, :], (species, lanes))
+                part = product[:, i * lanes : (i + 1) * lanes]
+                result = part[:species] + offb[0]
+                for e in range(1, entries):
+                    result = jnp.where(entry == e, part[e * species : (e + 1) * species] + offb[e], result)
+                results.append(jnp.maximum(result, 0.0))
+            states = [result.astype(bf16) for result in results]
         copies = []
-        for d in range(1, trc):
-            peer = lax.rem(me + d, trc)
-            copy = pltpu.make_async_remote_copy(
-                src_ref=rs.at[g, peer], dst_ref=back.at[g, me],
-                send_sem=ret_send.at[d - 1, g], recv_sem=ret_recv.at[d - 1, g],
-                device_id={"tile": me_tile, "trc": peer}, device_id_type=MESH,
-            )
-            copy.start()
-            copies.append(copy)
-        back[g, me] = rs[g, me]
+        for i, g in enumerate(group):
+            chem = jnp.where(sun, results[i], conc[i].astype(f32)).astype(bf16)
+            rs[g] = chem.reshape(trc, quarter, lanes)
+            for d in range(1, trc):
+                peer = lax.rem(me + d, trc)
+                copy = pltpu.make_async_remote_copy(
+                    src_ref=rs.at[g, peer], dst_ref=back.at[g, me],
+                    send_sem=ret_send.at[d - 1, g], recv_sem=ret_recv.at[d - 1, g],
+                    device_id={"tile": me_tile, "trc": peer}, device_id_type=MESH,
+                )
+                copy.start()
+                copies.append(copy)
+            back[g, me] = rs[g, me]
         return copies
 
-    sends = []
-    returns = []
-    for g in range(levels):
-        sends.append(cycle_level(g))
-        if g > 0:
-            returns.append(chem_level(g - 1, sends[g - 1]))
-    returns.append(chem_level(levels - 1, sends[levels - 1]))
+    sends = [cycle_level(g) for g in range(levels)]
+    returns = [chem_levels(range(g, min(g + 2, levels))) for g in range(0, levels, 2)]
 
     for copy in mixes:
         copy.wait()
@@ -300,7 +306,7 @@
                 xf[l * cols + c, rows, :] = current
         return 0
 
-    lax.fori_loop(0, chunks, solve_chunk, 0)
+    lax.fori_loop(0, chunks, solve_chunk, 0, unroll=2)
     stores = []
     for r in range(levels * cols):
         store = pltpu.make_async_copy(xf.at[r], out_hbm.at[:, r, 0, :], store_sem.at[r])
@@ -347,6 +353,7 @@
             pltpu.VMEM((entries, species, lanes), f32),
             pltpu.VMEM((4, levels, 8, lanes), f32),
             pltpu.VMEM((2, lanes, lanes), f32),
+            pltpu.VMEM((2, WIDTH, quarter, lanes), f32),
             pltpu.VMEM((rows, lanes), f32),
             pltpu.VMEM((rows, lanes), f32),
             pltpu.VMEM((substeps * levels, cols, lanes // trc), jnp.int32),

time: 34.6 us -> 27.1 us (0.78)
  Pallas kernels: 32.6 us -> 25 us
    pallas_call x1, Pallas kernels: 32.6 us -> 25 us  [shards(): pl.pallas_call(functools.partial(kernel, dims), out_shape=jax.ShapeDtypeS...]
where the time goes in v3:
time: 27.1 us; the launch traced here: 26.9 us
  Pallas kernels  25 us (92%)
  local copies, waits for them, and re-layouts  1.87 us (7%)
    pallas_call x1, Pallas kernels, shards(): pl.pallas_call(functools.partial(kernel, dims), out_shape=jax.ShapeDtypeS...  25 us
    unnamed x1, local copies, waits for them, and re-layouts  1.87 us

profile of v3, /device:TPU:0, one launch (start us, length us, event | category | flops | bytes accessed | tf_op | source)
XLA Modules:
  0.0 26.9 jit_solution(7149342361285643913)
XLA Ops:
  0.0 25.0 %shard_map.91 = f32[64,16,1,128]{3,2,1,0:T(1,128)} custom-call(f32[64,16,1,128]{3,2,1,0:T(1,128)} %bitcast.7, f32[16,128]{1,0:T(8,128)} %bitcast.10, f32[16,128]{1,0:T(8,128)} %bitcast.11, s32[1,2]{1,0:T(1,128)} %flag_ref.1, s32[16,4,32]{2,1,0:T(4,128)} %bitcast.9, s32[4,32]{1,0:T(4,128)} %sun_hbm.1, f32[3,4,32]{2,1,0:T(4,128)} %mix_hbm.1, ...), custom_call_target="tpu_custom_call" | custom-call | tf_op jit(solution)/shard_map/pallas_call | solution.py:334
  25.0 1.9 %copy.11 = f32[64,4,4,128]{3,2,1,0:T(4,128)} copy(f32[64,4,4,128]{3,2,1,0:T(4,128)} %bitcast.6) | data formatting | bytes 1048576

commit v4 on v3

--- a/solution.py
+++ b/solution.py
@@ -153,7 +153,7 @@
             yb[r, pl.ds(i * CHUNK, CHUNK), :] = cell + (flux - pltpu.roll(flux, lanes - 1, 1))
         return 0
 
-    lax.fori_loop(0, levels * cols, edge_row, 0, unroll=2)
+    lax.fori_loop(0, levels * cols, edge_row, 0, unroll=4)
 
     for e in range(entries):
         picked = lax.broadcasted_iota(jnp.int32, (entries, lanes), 0) == e
@@ -206,7 +206,7 @@
                 sb[g, p, rows, :] = moved[p].astype(bf16)
             return 0
 
-        lax.fori_loop(0, chunks, chunk, 0, unroll=2)
+        lax.fori_loop(0, chunks, chunk, 0, unroll=chunks)
         sends = []
         for d in range(1, trc):
             peer = lax.rem(me + d, trc)
@@ -306,12 +306,15 @@
                 xf[l * cols + c, rows, :] = current
         return 0
 
-    lax.fori_loop(0, chunks, solve_chunk, 0, unroll=2)
     stores = []
-    for r in range(levels * cols):
-        store = pltpu.make_async_copy(xf.at[r], out_hbm.at[:, r, 0, :], store_sem.at[r])
-        store.start()
-        stores.append(store)
+    half = chunks // 2
+    for part, (low, high) in enumerate(((0, half), (half, chunks))):
+        lax.fori_loop(low, high, solve_chunk, 0, unroll=2)
+        rows = pl.ds(low * CHUNK, (high - low) * CHUNK)
+        for r in range(levels * cols):
+            store = pltpu.make_async_copy(xf.at[r, rows], out_hbm.at[rows, r, 0, :], store_sem.at[part, r])
+            store.start()
+            stores.append(store)
     for group in halos + sends + returns:
         for copy in group:
             copy.wait_send()
@@ -366,7 +369,7 @@
             pltpu.VMEM((8, lanes), f32),
             dma((7,)),
             dma((rows,)),
-            dma((rows,)),
+            dma((2, rows)),
             dma((2, levels)),
             dma((2, levels)),
             dma,

time: 27.1 us -> 26.9 us (level)
  no operation moved by 1% of the time
where the time goes in v4:
time: 26.9 us; the launch traced here: 26.7 us
  Pallas kernels  24.8 us (92%)
  local copies, waits for them, and re-layouts  1.87 us (7%)
    pallas_call x1, Pallas kernels, shards(): pl.pallas_call(functools.partial(kernel, dims), out_shape=jax.ShapeDtypeS...  24.8 us
    unnamed x1, local copies, waits for them, and re-layouts  1.87 us

profile of v4, /device:TPU:0, one launch (start us, length us, event | category | flops | bytes accessed | tf_op | source)
XLA Modules:
  0.0 26.7 jit_solution(7154643281619184290)
XLA Ops:
  0.0 24.8 %shard_map.91 = f32[64,16,1,128]{3,2,1,0:T(1,128)} custom-call(f32[64,16,1,128]{3,2,1,0:T(1,128)} %bitcast.7, f32[16,128]{1,0:T(8,128)} %bitcast.10, f32[16,128]{1,0:T(8,128)} %bitcast.11, s32[1,2]{1,0:T(1,128)} %flag_ref.1, s32[16,4,32]{2,1,0:T(4,128)} %bitcast.9, s32[4,32]{1,0:T(4,128)} %sun_hbm.1, f32[3,4,32]{2,1,0:T(4,128)} %mix_hbm.1, ...), custom_call_target="tpu_custom_call" | custom-call | tf_op jit(solution)/shard_map/pallas_call | solution.py:337
  24.8 1.9 %copy.11 = f32[64,4,4,128]{3,2,1,0:T(4,128)} copy(f32[64,4,4,128]{3,2,1,0:T(4,128)} %bitcast.6) | data formatting | bytes 1048576
